TPU v7x, 512 devices: a whole 4x4x16 slice. The times are simulated.
512 devices in a mesh: dom: 128 (over z, y, core), feat: 4 (over x).
Axes of the slice: x: 4, y: 4, z: 16, core: 2. Of those that a mesh axis runs over, the one named last changes fastest.
Arguments:
- node_latent: bfloat16 [131072, 512], P(('dom', 'feat')), may hold values from -6 to 6
- edge_latent: bfloat16 [393216, 512], P(('dom', 'feat')), may hold values from -6 to 6
- weights: bfloat16 [7, 512, 512], P(None, 'feat'), may hold values from -0.1875 to 0.1875
- biases: float32 [4, 512], replicated, may hold values from -3 to 3
- gains: float32 [2, 512], replicated, may hold values from 0.1 to 1.9
- shifts: float32 [2, 512], replicated, may hold values from -3 to 3
- halo_send: int32 [128, 4, 64], P('dom'), may hold values from 0 to 1023
- halo_count: int32 [128, 4], P('dom'), may hold values from 1 to 64
- coarse_rows: int32 [128, 2], P('dom'), may hold values from 0 to 1023, as said below
- edge_send: int32 [393216], P(('dom', 'feat')), may hold values from 0 to 1535, as said below
- edge_recv: int32 [393216], P(('dom', 'feat')), may hold values from -1 to 127, as said below
- node_cot: bfloat16 [131072, 512], P(('dom', 'feat')), may hold values from -6 to 6
Outputs:
- node_out: bfloat16 [131072, 512], P(('dom', 'feat'))
- node_grad: float32 [131072, 512], P(('dom', 'feat'))
Inputs may be any that keep to these rules, and one draw needn't show every extreme that they name: `halo_send`: lists to the partitions at offsets +1, -1, +2, -2 of the sender, in that order; only the first halo_count entries of a list are live. `coarse_rows`: the rows of one partition are distinct. `edge_send`: A halo row of the table is named only if its slot is live. `edge_recv`: in each aligned block of 384 slots the live slots come first.
All inputs are finite; a program needn't handle non-finite values.
Results may differ from a plain program's by a relative error of at most 0.0051.
Values may be sent and summed in bfloat16 or wider, within the bound.
A program may use at most 64 MiB of HBM per device.

v0:
```python
import jax
import jax.numpy as jnp
from jax import lax
from jax.sharding import PartitionSpec as P

BLOCK = 128
EDGE_SLOTS = 384
SLOT = 64


OFFSETS = (1, -1, 2, -2)
epsilon = 1e-05


def shifted(block, axis, distance):
    devices = range(lax.axis_size(axis))
    route = [((i - distance) % len(devices), i) for i in devices]
    return lax.ppermute(block, axis, route)


def product(left, right):
    return jnp.dot(left, right, preferred_element_type=jnp.float32)


def silu_slope(values):
    sigmoid = jax.nn.sigmoid(values)
    return sigmoid * (1.0 + values * (1.0 - sigmoid))


def norm_forward(values, gain_row, shift_row):
    centre = jnp.mean(values, axis=-1, keepdims=True)
    centred = values - centre
    inv_std = lax.rsqrt(jnp.mean(centred * centred, axis=-1, keepdims=True) + epsilon)
    normed = centred * inv_std
    return (normed * gain_row + shift_row, normed, inv_std)


def norm_backward(upstream, normed, inv_std, gain_row):
    scaled = upstream * gain_row
    return inv_std * (
        scaled
        - jnp.mean(scaled, axis=-1, keepdims=True)
        - normed * jnp.mean(scaled * normed, axis=-1, keepdims=True)
    )


def body(
    node_latent,
    edge_latent,
    weights,
    biases,
    gains,
    shifts,
    halo_send,
    halo_count,
    coarse_rows,
    edge_send,
    edge_recv,
    node_cot,
):
    width = node_latent.shape[1]
    local_rows = node_latent.shape[0]
    edge_rows = edge_latent.shape[0]
    blocks = edge_rows // EDGE_SLOTS
    zero_half = jnp.zeros((), jnp.bfloat16)
    full_weights = lax.all_gather(weights, "feat", axis=1, tiled=True)
    w_edge = full_weights[0]
    w_send = full_weights[1]
    w_recv = full_weights[2]
    w_second = full_weights[3]
    w_node = full_weights[4]
    w_agg = full_weights[5]
    w_last = full_weights[6]
    send_local = product(node_latent, w_send).astype(jnp.bfloat16)
    recv_local = product(node_latent, w_recv).astype(jnp.bfloat16)
    part_table = lax.all_gather(send_local, "feat", axis=0, tiled=True)
    part_nodes = part_table.shape[0]
    own_send = halo_send[0]
    own_count = halo_count[0]
    slot_iota = jnp.arange(SLOT, dtype=jnp.int32)
    arrived = []
    for order in range(4):
        outgoing = jnp.where(
            (slot_iota < own_count[order])[:, None], part_table[own_send[order]], zero_half
        )
        arrived.append(shifted(outgoing, "dom", OFFSETS[order]))
    halo_table = jnp.concatenate(arrived, axis=0)
    coarse_mine = part_table[coarse_rows[0]]
    coarse_table = lax.all_gather(coarse_mine, "dom", axis=0, tiled=True)
    table = jnp.concatenate([part_table, halo_table, coarse_table], axis=0)
    table_rows = table.shape[0]
    send_term = table[edge_send]
    onehot = (
        edge_recv.reshape(blocks, EDGE_SLOTS)[:, :, None]
        == jnp.arange(BLOCK, dtype=jnp.int32)[None, None, :]
    ).astype(jnp.bfloat16)
    recv_term = jnp.einsum(
        "bej,bjd->bed",
        onehot,
        recv_local.reshape(blocks, BLOCK, width),
        preferred_element_type=jnp.float32,
    ).reshape(edge_rows, width)
    hidden_in = product(edge_latent, w_edge) + send_term.astype(jnp.float32) + recv_term + biases[0]
    edge_act = jax.nn.silu(hidden_in).astype(jnp.bfloat16)
    edge_pre = product(edge_act, w_second) + biases[1]
    message_full, edge_normed, edge_inv = norm_forward(edge_pre, gains[0], shifts[0])
    message = message_full.astype(jnp.bfloat16)
    aggregate = (
        jnp.einsum(
            "bej,bed->bjd",
            onehot,
            message.reshape(blocks, EDGE_SLOTS, width),
            preferred_element_type=jnp.float32,
        )
        .astype(jnp.bfloat16)
        .reshape(local_rows, width)
    )
    node_in = product(node_latent, w_node) + product(aggregate, w_agg) + biases[2]
    node_act = jax.nn.silu(node_in).astype(jnp.bfloat16)
    node_pre = product(node_act, w_last) + biases[3]
    update, node_normed, node_inv = norm_forward(node_pre, gains[1], shifts[1])
    node_out = (node_latent.astype(jnp.float32) + update).astype(jnp.bfloat16)
    cot_float = node_cot.astype(jnp.float32)
    node_back = norm_backward(cot_float, node_normed, node_inv, gains[1]).astype(jnp.bfloat16)
    node_in_grad = (product(node_back, w_last.T) * silu_slope(node_in)).astype(jnp.bfloat16)
    agg_grad = product(node_in_grad, w_agg.T).astype(jnp.bfloat16)
    message_grad = jnp.einsum(
        "bej,bjd->bed",
        onehot,
        agg_grad.reshape(blocks, BLOCK, width),
        preferred_element_type=jnp.float32,
    ).reshape(edge_rows, width)
    edge_back = norm_backward(message_grad, edge_normed, edge_inv, gains[0]).astype(jnp.bfloat16)
    hidden_grad = (product(edge_back, w_second.T) * silu_slope(hidden_in)).astype(jnp.bfloat16)
    table_grad = jax.ops.segment_sum(
        hidden_grad.astype(jnp.float32), edge_send, num_segments=table_rows
    )
    recv_grad = (
        jnp.einsum(
            "bej,bed->bjd",
            onehot,
            hidden_grad.reshape(blocks, EDGE_SLOTS, width),
            preferred_element_type=jnp.float32,
        )
        .astype(jnp.bfloat16)
        .reshape(local_rows, width)
    )
    halo_grad = table_grad[part_nodes : part_nodes + 4 * SLOT].reshape(4, SLOT, width)
    coarse_grad = table_grad[part_nodes + 4 * SLOT :]
    coarse_back = lax.psum_scatter(coarse_grad, "dom", scatter_dimension=0, tiled=True)
    returned_list = []
    for order in range(4):
        returned = shifted(halo_grad[order].astype(jnp.bfloat16), "dom", -OFFSETS[order]).astype(
            jnp.float32
        )
        returned_list.append(jnp.where((slot_iota < own_count[order])[:, None], returned, 0.0))
    returned_values = jnp.concatenate(returned_list + [coarse_back], axis=0)
    returned_index = jnp.concatenate([own_send.reshape(-1), coarse_rows[0]], axis=0)
    part_grad = table_grad[:part_nodes].at[returned_index].add(returned_values)
    send_grad = lax.psum_scatter(
        part_grad.astype(jnp.bfloat16), "feat", scatter_dimension=0, tiled=True
    )
    node_grad = (
        cot_float
        + product(node_in_grad, w_node.T)
        + product(send_grad, w_send.T)
        + product(recv_grad, w_recv.T)
    )
    return (node_out, node_grad)


def solution(mesh):
    return jax.shard_map(
        body,
        mesh=mesh,
        in_specs=(
            P(("dom", "feat"), None),
            P(("dom", "feat"), None),
            P(None, "feat", None),
            P(),
            P(),
            P(),
            P("dom", None, None),
            P("dom", None),
            P("dom", None),
            P(("dom", "feat")),
            P(("dom", "feat")),
            P(("dom", "feat"), None),
        ),
        out_specs=(P(("dom", "feat"), None), P(("dom", "feat"), None)),
        check_vma=False,
    )
```

profile of v0, /device:TPU:1, one launch (start us, length us, event | category | flops | bytes accessed | tf_op | source)
XLA Modules:
  0.0 639.2 jit_solution(13523650680208287682)
XLA Ops:
  15.6 51.4 %all-gather.5.cloned.1.call-done = bf16[7,512,512]{2,1,0:T(8,128)(2,1)} async-done(((bf16[7,128,512]{2,1,0:T(8,128)(2,1)}), bf16[7,512,512]{2,1,0:T(8,128)(2,1)}) %all-gather.5.cloned.1.call-update) | async-done | bytes 3670032 | tf_op jit(solution)/shard_map/all_gather | solution.py:66
  67.0 2.1 convolution_convert_fusion.2
  72.4 2.1 fusion.14
  76.1 2.8 fusion.13
  78.9 22.0 %all-gather.7.cloned.1.call-done = bf16[1024,512]{1,0:T(8,128)(2,1)} async-done(((bf16[256,512]{1,0:T(8,128)(2,1)}), bf16[1024,512]{1,0:T(8,128)(2,1)}) %all-gather.7.cloned.1.call-update) | async-done | bytes 1048592 | tf_op jit(solution)/shard_map/all_gather | solution.py:76
  100.8 2.2 gather_fusion
  103.1 4.6 collective-permute-start
  107.7 2.1 gather_fusion.1
  113.8 3.1 collective-permute-start.2
  118.3 5.6 collective-permute-start.3
  125.2 103.9 %all-gather.1 = bf16[128,2,512]{2,1,0:T(2,128)(2,1)S(1)} all-gather(bf16[1,2,512]{2,1,0:T(2,128)(2,1)} %bitcast.106), channel_id=2, replica_groups=mesh['dom'=128,'feat'=4] {'dom'}, dimensions={0}, use_global_device_ids=true | all-gather | bytes 264192 | tf_op jit(solution)/shard_map/all_gather | solution.py:89
  231.8 2.7 gather_fusion.5
  234.6 2.5 fusion
  244.7 1.9 multiply_reduce_fusion
  250.0 8.8 %scatter_custom_fusion = f32[1536,512]{1,0:T(8,128)} fusion(s32[768]{0:T(1024)} %param.21, bf16[768,512]{1,0:T(8,128)(2,1)S(1)} %multiply_convert_fusion, f32[]{:T(128)} %constant.15.clone.1), kind=kCustom, calls=%fused_computation.11 | custom fusion | flops 786432 | bytes 3932672 | tf_op jit(solution)/shard_map/scatter-add | solution.py:135
  258.8 2.1 convert.6
  261.6 2.1 collective-permute-start.4
  267.7 3.3 collective-permute-start.7
  271.0 5.6 collective-permute-start.6
  279.9 2.8 collective-permute-done.5
  285.6 310.5 %all-reduce.3.cloned.1.call-done = f32[256,512]{1,0:T(8,128)} async-done(((f32[256,512]{1,0:T(8,128)}), f32[256,512]{1,0:T(8,128)}) %all-reduce.3.cloned.1.call-update) | async-done | bytes 524304
  597.3 3.4 scatter_fusion
  604.7 24.4 %reduce-scatter.2.cloned.1.call-done = bf16[256,512]{1,0:T(8,128)(2,1)} async-done(((bf16[1024,512]{1,0:T(8,128)(2,1)}), bf16[256,512]{1,0:T(8,128)(2,1)}) %reduce-scatter.2.cloned.1.call-update) | async-done | bytes 262160 | tf_op jit(solution)/shard_map/reduce_scatter | solution.py:160
  630.5 2.2 convolution_add_fusion.1
  (143 shorter events, 50.2 us)
Async XLA Ops:
  7.2 68.9 %copy-start = (bf16[768,512]{1,0:T(8,128)(2,1)S(1)}, bf16[768,512]{1,0:T(8,128)(2,1)}, u32[]{:S(2)}) copy-start(bf16[768,512]{1,0:T(8,128)(2,1)} %param.13) | copy-start | bytes 2359300
  7.2 63.9 %copy-start.8 = (bf16[256,512]{1,0:T(8,128)(2,1)S(1)}, bf16[256,512]{1,0:T(8,128)(2,1)}, u32[]{:S(2)}) copy-start(bf16[256,512]{1,0:T(8,128)(2,1)} %param.12) | copy-start | bytes 786436
  7.2 62.6 %copy-start.17 = (s32[768]{0:T(1024)S(1)}, s32[768]{0:T(1024)}, u32[]{:S(2)}) copy-start(s32[768]{0:T(1024)} %param.22) | copy-start | bytes 9220
  7.2 62.6 %copy-start.18 = (f32[2,512]{1,0:T(2,128)S(1)}, f32[2,512]{1,0:T(2,128)}, u32[]{:S(2)}) copy-start(f32[2,512]{1,0:T(2,128)} %param.17) | copy-start | bytes 12292
  7.2 63.2 %copy-start.14 = (f32[4,512]{1,0:T(4,128)S(1)}, f32[4,512]{1,0:T(4,128)}, u32[]{:S(2)}) copy-start(f32[4,512]{1,0:T(4,128)} %param.15) | copy-start | bytes 24580
  7.2 59.8 %all-gather.5.cloned.1.call-start = ((), (), s32[]{:S(2)}) async-start(), calls=%async_computation.1 | async-start | bytes 4587520 | tf_op jit(solution)/shard_map/all_gather | solution.py:66
  8.0 92.9 %all-gather.7.cloned.1.call-start = ((), (), s32[]{:S(2)}) async-start(), calls=%async_computation.2 | async-start | bytes 1310720 | tf_op jit(solution)/shard_map/all_gather | solution.py:76
  10.1 107.5 %copy-start.19 = (pred[64]{0:T(512)(128)(4,1)}, pred[64]{0:T(512)(128)(4,1)S(1)}, u32[]{:S(2)}) copy-start(pred[64]{0:T(512)(128)(4,1)S(1)} %iota_compare_fusion.5) | copy-start | bytes 196
  10.8 99.0 %copy-start.21 = (pred[64]{0:T(512)(128)(4,1)}, pred[64]{0:T(512)(128)(4,1)S(1)}, u32[]{:S(2)}) copy-start(pred[64]{0:T(512)(128)(4,1)S(1)} %iota_compare_fusion.7) | copy-start | bytes 196
  11.4 91.6 %copy-start.23 = (pred[64]{0:T(512)(128)(4,1)}, pred[64]{0:T(512)(128)(4,1)S(1)}, u32[]{:S(2)}) copy-start(pred[64]{0:T(512)(128)(4,1)S(1)} %iota_compare_fusion.8) | copy-start | bytes 196
  69.2 526.9 %all-reduce.3.cloned.1.call-start = ((), (), s32[]{:S(2)}) async-start(), calls=%async_computation.4 | async-start | bytes 1048576
  69.8 43.3 %copy-start.24 = (pred[64]{0:T(512)(128)(4,1)}, pred[64]{0:T(512)(128)(4,1)S(1)}, u32[]{:S(2)}) copy-start(pred[64]{0:T(512)(128)(4,1)S(1)} %iota_compare_fusion.6) | copy-start | bytes 196
  103.1 126.2 %collective-permute-start = (bf16[64,512]{1,0:T(8,128)(2,1)S(1)}, bf16[64,512]{1,0:T(8,128)(2,1)S(1)}, u32[]{:S(2)}, u32[]{:S(2)}) collective-permute-start(bf16[64,512]{1,0:T(8,128)(2,1)S(1)} %broadcast_select_fusion.3), channel_id=1, source_target_pairs={{508,0},{0,4},{4,8},{8,12},{12,16},{16,20},{20,24},{24,28},{28,32}... | collective-permute-start | bytes 196616 | tf_op jit(solution)/shard_map/ppermute | solution.py:18
  110.5 118.8 %collective-permute-start.1 = (bf16[64,512]{1,0:T(8,128)(2,1)}, bf16[64,512]{1,0:T(8,128)(2,1)}, u32[]{:S(2)}, u32[]{:S(2)}) collective-permute-start(bf16[64,512]{1,0:T(8,128)(2,1)} %broadcast_select_fusion.2), channel_id=1, source_target_pairs={{4,0},{8,4},{12,8},{16,12},{20,16},{24,20},{28,24},{32,28},{36,32}... | collective-permute-start | bytes 196616 | tf_op jit(solution)/shard_map/ppermute | solution.py:18
  113.8 116.3 %collective-permute-start.2 = (bf16[64,512]{1,0:T(8,128)(2,1)}, bf16[64,512]{1,0:T(8,128)(2,1)}, u32[]{:S(2)}, u32[]{:S(2)}) collective-permute-start(bf16[64,512]{1,0:T(8,128)(2,1)} %broadcast_select_fusion.1), channel_id=1, source_target_pairs={{504,0},{508,4},{0,8},{4,12},{8,16},{12,20},{16,24},{20,28},{24,32... | collective-permute-start | bytes 196616 | tf_op jit(solution)/shard_map/ppermute | solution.py:18
  118.3 112.7 %collective-permute-start.3 = (bf16[64,512]{1,0:T(8,128)(2,1)}, bf16[64,512]{1,0:T(8,128)(2,1)}, u32[]{:S(2)}, u32[]{:S(2)}) collective-permute-start(bf16[64,512]{1,0:T(8,128)(2,1)} %broadcast_select_fusion), channel_id=1, source_target_pairs={{8,0},{12,4},{16,8},{20,12},{24,16},{28,20},{32,24},{36,28},{40,32... | collective-permute-start | bytes 196616 | tf_op jit(solution)/shard_map/ppermute | solution.py:18
  261.6 17.0 %collective-permute-start.4 = (bf16[64,512]{1,0:T(8,128)(2,1)}, bf16[64,512]{1,0:T(8,128)(2,1)S(1)}, u32[]{:S(2)}, u32[]{:S(2)}) collective-permute-start(bf16[64,512]{1,0:T(8,128)(2,1)} %get-tuple-element.7), channel_id=1, source_target_pairs={{4,0},{8,4},{12,8},{16,12},{20,16},{24,20},{28,24},{32,28},{36,32}... | collective-permute-start | bytes 196616 | tf_op jit(solution)/shard_map/ppermute | solution.py:18
  267.6 15.1 %copy-start.22 = (pred[64]{0:T(512)(128)(4,1)S(1)}, pred[64]{0:T(512)(128)(4,1)}, u32[]{:S(2)}) copy-start(pred[64]{0:T(512)(128)(4,1)} %copy-done.21) | copy-start | bytes 196
  267.6 17.2 %copy-start.20 = (pred[64]{0:T(512)(128)(4,1)S(1)}, pred[64]{0:T(512)(128)(4,1)}, u32[]{:S(2)}) copy-start(pred[64]{0:T(512)(128)(4,1)} %copy-done.19) | copy-start | bytes 196
  267.6 329.7 %slice-start = ((f32[1536,512]{1,0:T(8,128)}), f32[1024,512]{1,0:T(8,128)S(1)}, s32[]{:S(2)}) async-start(f32[1536,512]{1,0:T(8,128)} %scatter_custom_fusion), calls=%async_computation.5 | async-start | bytes 4194304 | tf_op jit(solution)/shard_map/slice | solution.py:159
  267.7 361.4 %reduce-scatter.2.cloned.1.call-start = ((), (), s32[]{:S(2)}) async-start(), calls=%async_computation.3 | async-start | bytes 1310720 | tf_op jit(solution)/shard_map/reduce_scatter | solution.py:160
  267.7 17.1 %collective-permute-start.7 = (bf16[64,512]{1,0:T(8,128)(2,1)S(1)}, bf16[64,512]{1,0:T(8,128)(2,1)S(1)}, u32[]{:S(2)}, u32[]{:S(2)}) collective-permute-start(bf16[64,512]{1,0:T(8,128)(2,1)S(1)} %get-tuple-element.4), channel_id=1, source_target_pairs={{504,0},{508,4},{0,8},{4,12},{8,16},{12,20},{16,24},{20,28},{24,32... | collective-permute-start | bytes 196616 | tf_op jit(solution)/shard_map/ppermute | solution.py:18
  271.0 12.4 %collective-permute-start.6 = (bf16[64,512]{1,0:T(8,128)(2,1)}, bf16[64,512]{1,0:T(8,128)(2,1)S(1)}, u32[]{:S(2)}, u32[]{:S(2)}) collective-permute-start(bf16[64,512]{1,0:T(8,128)(2,1)} %get-tuple-element.5), channel_id=1, source_target_pairs={{8,0},{12,4},{16,8},{20,12},{24,16},{28,20},{32,24},{36,28},{40,32... | collective-permute-start | bytes 196616 | tf_op jit(solution)/shard_map/ppermute | solution.py:18
  276.7 6.0 collective-permute-start.5
  (17 other events, 50.5 us)
Sparse Core Ops, SparseCore 0:
  10.2 56.8 all-gather.4
  69.7 31.0 all-gather.6
  267.8 328.1 all-reduce.2
  602.0 27.0 reduce-scatter.1
where the time goes:
time: 642 us; the launch traced here: 639 us
  waiting for transfers between devices  412 us (64%)
  blocking collectives  104 us (16%)
  other arithmetic  33.8 us (5%)
  starting transfers between devices  28.2 us (4%)
  local copies, waits for them, and re-layouts  24.1 us (4%)
  matrix products  22.4 us (3%)
  between operations  15 us (2%)
    unnamed x5, waiting for transfers between devices  311 us
    all_gather x1, blocking collectives, body(): coarse_table = lax.all_gather(coarse_mine, 'dom', axis=0, tiled=True)  104 us
    all_gather x1, waiting for transfers between devices, body(): full_weights = lax.all_gather(weights, 'feat', axis=1, tiled=True)  51.4 us
    ppermute x8, starting transfers between devices, shifted(): return lax.ppermute(block, axis, route)  28.1 us
    reduce_scatter x1, waiting for transfers between devices, body(): lax.psum_scatter(part_grad.astype(jnp.bfloat16), 'feat', scatter_dimensio...  24.4 us
    all_gather x1, waiting for transfers between devices, body(): part_table = lax.all_gather(send_local, 'feat', axis=0, tiled=True)  22 us
    dot_general x13, matrix products, product(): return jnp.dot(left, right, preferred_element_type=jnp.float32)  17.5 us
  transfers between devices with their start and end apart: 12, of which 5 were waited for; matrix products, arithmetic and copies ran while one was open for 6% of the time, Pallas kernels for 0%

commit v1 on v0

v1 whole, which is shorter than its diff:
```python
import jax
import jax.numpy as jnp
from jax import lax
from jax.experimental import pallas as pl
from jax.experimental.pallas import tpu as pltpu
from jax.sharding import PartitionSpec as P

MESH = pl.DeviceIdType.MESH
F32, BF16 = jnp.float32, jnp.bfloat16
D = 512
ROWS = 256
EDGES = 768
BLOCK = 128
SLOTS = 384
PART = 1024
HALO = 256
COARSE = 256
TABLE = PART + HALO + COARSE
OFFSETS = (1, -1, 2, -2)
NZ, NY, NX = 16, 4, 4
GROUPS = ((0, 3), (3, 4))
EPS = 1e-05

COUNTS = dict(c1=3, w1=12, lat=3, c2=15, w2=12, halo=4, w3=4, c3=7, hb=4, rs=3, rc1=7, rc2=15, rc3=3)
BASE = {}
_total = 0
for _name, _n in COUNTS.items():
    BASE[_name] = _total
    _total += _n
N_SEM = _total


def dot(a, b):
    return jnp.dot(a, b, preferred_element_type=F32)


def dot_t(a, b):
    return lax.dot_general(a, b, (((1,), (1,)), ((), ())), preferred_element_type=F32)


def sigmoid(v):
    return 1.0 / (1.0 + jnp.exp(-v))


def onehot(mask):
    return jnp.where(mask, 1.0, 0.0).astype(BF16)


def iota(shape, dim):
    return lax.broadcasted_iota(jnp.int32, shape, dim)


def columns(row):
    wide = jnp.broadcast_to(row.astype(F32), (128, row.shape[1]))
    return wide.T.astype(jnp.int32)


def norm(values):
    centred = values - jnp.mean(values, axis=-1, keepdims=True)
    inv = lax.rsqrt(jnp.mean(centred * centred, axis=-1, keepdims=True) + EPS)
    return centred * inv, inv


def norm_back(scaled, normed, inv):
    return inv * (
        scaled
        - jnp.mean(scaled, axis=-1, keepdims=True)
        - normed * jnp.mean(scaled * normed, axis=-1, keepdims=True)
    )


def kernel(
    coarse_ref, count_ref, node_ref, edge_ref, wsh_ref, bias_ref, gain_ref, shift_ref,
    halo_ref, esend_ref, erecv_ref, cot_ref,
    out_ref, grad_ref,
    lat, tab, w, sel, sel_t, rsel, rsel_t, hid, normed_e, inv_e, msg, hg,
    c1_src, c1_buf, c2_src, c2_buf, c3_src, halo_src, hb_src, hb_buf, part_src, rs_buf,
    rc1_src, rc1_buf, rc2_src, rc2_buf, rc3_src, rc3_buf,
    send_sem, recv_sem, local_sem,
):
    dom, x = lax.axis_index("dom"), lax.axis_index("feat")
    z, y, c = dom // 8, (dom // 2) % 4, dom % 2
    yc = dom % 8
    zm = z % 4

    def at_x(d):
        return (dom, (x + d) % NX)

    def at_z(d):
        return (((z + d + NZ) % NZ) * 8 + yc, x)

    def at_y(d):
        return (z * 8 + ((y + d) % NY) * 2 + c, x)

    def at_yc(e):
        return (z * 8 + (yc + e) % 8, x)

    def at_dom(o):
        return ((dom + o + 128) % 128, x)

    other_core = (z * 8 + y * 2 + (1 - c), x)

    def copy(name, number, src, dst, device):
        at = BASE[name] + number
        return pltpu.make_async_remote_copy(
            src_ref=src, dst_ref=dst, send_sem=send_sem.at[at], recv_sem=recv_sem.at[at],
            device_id=device, device_id_type=MESH,
        )

    barrier = pltpu.get_barrier_semaphore()
    for d in (1, 2, 3):
        pl.semaphore_signal(barrier, inc=1, device_id=at_x(d), device_id_type=MESH)
    for e in range(1, 8):
        pl.semaphore_signal(barrier, inc=1, device_id=at_yc(e), device_id_type=MESH)
    for o in OFFSETS:
        pl.semaphore_signal(barrier, inc=1, device_id=at_dom(o), device_id_type=MESH)

    def greet(d, carry):
        pl.semaphore_signal(barrier, inc=1, device_id=at_z(d), device_id_type=MESH)
        return carry

    lax.fori_loop(1, NZ, greet, 0)

    row8 = iota((8, ROWS), 0)
    wanted = jnp.where(row8 % 2 == 0, coarse_ref[0, 0], coarse_ref[0, 1]) - x * ROWS
    picked = dot(onehot(wanted == iota((8, ROWS), 1)), node_ref[...])
    quarter = iota((8, 128), 0) // 2
    tile = jnp.zeros((8, 128), F32)
    for j in range(4):
        tile = jnp.where(quarter == j, picked[:, 128 * j : 128 * j + 128], tile)
    c1_src[...] = tile

    own_rows = pl.ds(pl.multiple_of(x * ROWS, ROWS), ROWS)
    lat[own_rows, :] = node_ref[...]
    pl.semaphore_wait(barrier, 3 + 7 + 4 + 15)

    c1 = [copy("c1", d - 1, c1_src, c1_buf.at[d - 1], at_x(d)) for d in (1, 2, 3)]
    for one in c1:
        one.start()
    pieces = ((y, 0), (zm, 1))
    w1 = {}
    for g, (first, count) in enumerate(GROUPS):
        mats = pl.ds(first, count)
        for t, (j, _) in enumerate(pieces):
            cols = pl.ds(256 * t, 256)
            for d in (2, 1, 3):
                w1[g, t, d] = copy(
                    "w1", (g * 2 + t) * 3 + d - 1,
                    wsh_ref.at[mats, j, c, :, cols], w.at[mats, x, j, c, :, cols], at_x(d),
                )
                w1[g, t, d].start()
    lat_copies = [copy("lat", d - 1, node_ref, lat.at[own_rows, :], at_x(d)) for d in (2, 1, 3)]
    for one in lat_copies:
        one.start()
    for t, (j, _) in enumerate(pieces):
        cols = pl.ds(256 * t, 256)
        own = pltpu.make_async_copy(
            wsh_ref.at[:, j, c, :, cols], w.at[:, x, j, c, :, cols], local_sem.at[t]
        )
        own.start()
        own.wait()

    halo_row = halo_ref[...]
    lane = iota((1, HALO), 1)
    live = count_ref[0, 0]
    for k in (1, 2, 3):
        live = jnp.where(lane // 64 == k, count_ref[0, k], live)
    halo_row = jnp.where(lane % 64 < live, halo_row, -1)
    halo_col = columns(halo_row)

    for one in c1:
        one.wait_recv()
    total = c1_src[...] + c1_buf[0] + c1_buf[1] + c1_buf[2]
    c2_src[...] = total
    c2_buf[z] = total

    def c2(d):
        at = BASE["c2"] + d - 1
        return pltpu.make_async_remote_copy(
            src_ref=c2_src, dst_ref=c2_buf.at[z],
            send_sem=send_sem.at[at], recv_sem=recv_sem.at[at],
            device_id=at_z(d), device_id_type=MESH,
        )

    order = [8]
    for i in range(1, 8):
        order += [8 - i, 8 + i]
    for d in order:
        c2(d).start()

    index = esend_ref[...]
    m = index - (PART + HALO)
    index = jnp.where(
        m >= 0, PART + HALO + ((m >> 1) & 7) * 32 + (m >> 4) * 2 + (m & 1), index
    )

    def w2_start(g):
        first, count = GROUPS[g]
        mats = pl.ds(first, count)
        started = []
        for t, (j, _) in enumerate(pieces):
            cols = pl.ds(256 * t, 256)
            for d in (1, 2, 3):
                w1[g, t, d].wait_recv()
            for d in (2, 1, 3):
                step = d if d < 3 else -1
                target = at_y(d) if t == 0 else at_z(step)
                part = w.at[mats, :, j, c, :, cols]
                one = copy("w2", (g * 2 + t) * 3 + d - 1, part, part, target)
                one.start()
                started.append(one)
        return started

    def w3_start(g, arrived):
        first, count = GROUPS[g]
        mats = pl.ds(first, count)
        started = []
        for t in range(2):
            for one in arrived[3 * t : 3 * t + 3]:
                one.wait_recv()
            part = w.at[mats, :, :, c, :, pl.ds(256 * t, 256)]
            one = copy("w3", g * 2 + t, part, part, other_core)
            one.start()
            started.append(one)
        return started

    w2a = w2_start(0)
    index_col = columns(index)
    for j in range(TABLE // 128):
        sel[:, 128 * j : 128 * j + 128] = onehot(index_col == iota((EDGES, 128), 1) + 128 * j)
    w2b = w2_start(1)
    recv_row = erecv_ref[...]
    recv_col = columns(recv_row)
    rsel[...] = onehot(recv_col == iota((EDGES, 128), 1))
    for b in range(2):
        rsel_t[b] = onehot(
            iota((BLOCK, SLOTS), 0) == recv_row[:, SLOTS * b : SLOTS * b + SLOTS]
        )

    w3a = w3_start(0, w2a)
    for one in lat_copies:
        one.wait_recv()
    chosen = jnp.zeros((HALO, D), F32)
    for j in range(2):
        pick = jnp.concatenate(
            [onehot(halo_col == iota((HALO, 128), 1) + 128 * (4 * j + i)) for i in range(4)], axis=1
        )
        chosen += dot(pick, lat[512 * j : 512 * j + 512, :])
    halo_src[...] = chosen.astype(BF16)
    halo_copies = []
    for k in range(4):
        one = copy(
            "halo", k, halo_src.at[pl.ds(64 * k, 64)], lat.at[pl.ds(PART + 64 * k, 64)], at_dom(OFFSETS[k])
        )
        one.start()
        halo_copies.append(one)

    for d in order:
        c2(d).wait_recv()
    flat = c2_buf[...].reshape(NZ * 8, 128).astype(BF16)
    parts = []
    for j in range(4):
        row = iota((32, 128), 0)
        parts.append(dot(onehot((row // 2) * 8 + 2 * j + row % 2 == iota((32, 128), 1)), flat))
    own_coarse = jnp.concatenate(parts, axis=1).astype(BF16)
    c3_src[...] = own_coarse
    coarse_rows = pl.ds(pl.multiple_of(PART + HALO + yc * 32, 32), 32)
    lat[coarse_rows, :] = own_coarse
    c3 = [copy("c3", e - 1, c3_src, lat.at[coarse_rows, :], at_yc(e)) for e in range(1, 8)]
    for one in c3:
        one.start()
    w3b = w3_start(1, w2b)

    def weight(i):
        return w[i].reshape(D, D)

    for one in w3a:
        one.wait_recv()
    w_e, w_s, w_r = weight(0), weight(1), weight(2)
    recv_proj = dot(node_ref[...], w_r).astype(BF16)
    for j in range(4):
        rows = slice(256 * j, 256 * j + 256)
        tab[rows, :] = dot(lat[rows, :], w_s).astype(BF16)
    for b in range(2):
        rows = slice(SLOTS * b, SLOTS * b + SLOTS)
        hid[rows, :] = (
            dot(edge_ref[rows, :], w_e)
            + dot(rsel[rows, :], recv_proj[BLOCK * b : BLOCK * b + BLOCK])
            + dot(sel[rows, :PART], tab[:PART, :])
            + bias_ref[0:1, :]
        )
    for j in range(TABLE // 128):
        sel_t[128 * j : 128 * j + 128, :] = onehot(iota((128, EDGES), 0) + 128 * j == index)
    for one in halo_copies:
        one.wait_recv()
    rows = slice(PART, PART + HALO)
    tab[rows, :] = dot(lat[rows, :], w_s).astype(BF16)
    for one in c3:
        one.wait_recv()
    rows = slice(PART + HALO, TABLE)
    tab[rows, :] = dot(lat[rows, :], w_s).astype(BF16)

    for one in w3b:
        one.wait_recv()
    aggregate = []
    for b in range(2):
        rows = slice(SLOTS * b, SLOTS * b + SLOTS)
        h = hid[rows, :] + dot(sel[rows, PART:], tab[PART:, :])
        hid[rows, :] = h
        act = (h * sigmoid(h)).astype(BF16)
        normed, inv = norm(dot(act, weight(3)) + bias_ref[1:2, :])
        normed_e[rows, :] = normed
        inv_e[rows, :] = inv
        msg[rows, :] = (normed * gain_ref[0:1, :] + shift_ref[0:1, :]).astype(BF16)
        aggregate.append(dot(rsel_t[b], msg[rows, :]).astype(BF16))
    aggregate = jnp.concatenate(aggregate, axis=0)
    node = node_ref[...]
    node_in = dot(node, weight(4)) + dot(aggregate, weight(5)) + bias_ref[2:3, :]
    s = sigmoid(node_in)
    slope = s * (1.0 + node_in * (1.0 - s))
    normed, inv = norm(dot((node_in * s).astype(BF16), weight(6)) + bias_ref[3:4, :])
    out_ref[...] = (
        node.astype(F32) + (normed * gain_ref[1:2, :] + shift_ref[1:2, :])
    ).astype(BF16)
    cot = cot_ref[...].astype(F32)
    node_back = norm_back(cot * gain_ref[1:2, :], normed, inv).astype(BF16)
    node_in_grad = (dot_t(node_back, weight(6)) * slope).astype(BF16)
    agg_grad = dot_t(node_in_grad, weight(5)).astype(BF16)
    for b in range(2):
        rows = slice(SLOTS * b, SLOTS * b + SLOTS)
        back = dot(rsel[rows, :], agg_grad[BLOCK * b : BLOCK * b + BLOCK])
        edge_back = norm_back(back * gain_ref[0:1, :], normed_e[rows, :], inv_e[rows, :]).astype(BF16)
        h = hid[rows, :]
        s = sigmoid(h)
        hg[rows, :] = (dot_t(edge_back, weight(3)) * (s * (1.0 + h * (1.0 - s)))).astype(BF16)

    rc1_src[...] = dot(sel_t[PART + HALO :, :], hg[...]).astype(BF16)
    rc1 = [
        copy(
            "rc1", e - 1,
            rc1_src.at[pl.ds(pl.multiple_of((yc + e) % 8 * 32, 32), 32)], rc1_buf.at[e - 1], at_yc(e),
        )
        for e in range(1, 8)
    ]
    for one in rc1:
        one.start()
    hb_src[...] = dot(sel_t[PART : PART + HALO, :], hg[...]).astype(BF16)
    hb = []
    for k in range(4):
        part = pl.ds(64 * k, 64)
        hb.append(copy("hb", k, hb_src.at[part], hb_buf.at[part], at_dom(-OFFSETS[k])))
        hb[-1].start()

    recv_grad = [
        dot(rsel_t[b], hg[SLOTS * b : SLOTS * b + SLOTS, :]).astype(BF16) for b in range(2)
    ]
    grad_ref[...] = (
        cot_ref[...].astype(F32)
        + dot_t(node_in_grad, weight(4))
        + dot_t(jnp.concatenate(recv_grad, axis=0), weight(2))
    )

    for one in rc1:
        one.wait_recv()
    gathered = rc1_src[pl.ds(pl.multiple_of(yc * 32, 32), 32), :].astype(F32)
    for e in range(7):
        gathered += rc1_buf[e].astype(F32)
    gathered = gathered.astype(BF16)
    spread = jnp.zeros((NZ * 8, 128), F32)
    for j in range(4):
        row, col = iota((NZ * 8, 32), 0), iota((NZ * 8, 32), 1)
        place = (row // 8 == col // 2) & (row % 8 == 2 * j + col % 2)
        spread += dot(onehot(place), gathered[:, 128 * j : 128 * j + 128])
    rc2_src[...] = spread.reshape(NZ, 8, 128)
    rc2_buf[z] = rc2_src[z]

    def rc2(d):
        at = BASE["rc2"] + d - 1
        return pltpu.make_async_remote_copy(
            src_ref=rc2_src.at[(z + d) % NZ], dst_ref=rc2_buf.at[z],
            send_sem=send_sem.at[at], recv_sem=recv_sem.at[at],
            device_id=at_z(d), device_id_type=MESH,
        )

    for d in order:
        rc2(d).start()

    for one in hb:
        one.wait_recv()
    rs = []
    for d in (2, 1, 3, 0):
        start_row = pl.multiple_of(((x + d) % NX) * ROWS, ROWS)
        chunk = pl.ds(start_row, ROWS)
        place = onehot(iota((ROWS, HALO), 0) + start_row == halo_row)
        value = dot(sel_t[chunk, :], hg[...]) + dot(place, hb_buf[...])
        if d:
            part_src[d - 1] = value.astype(BF16)
            rs.append(copy("rs", d - 1, part_src.at[d - 1], rs_buf.at[d - 1], at_x(d)))
            rs[-1].start()
        else:
            hid[:ROWS, :] = value

    for d in order:
        rc2(d).wait_recv()
    tile = jnp.sum(rc2_buf[...], axis=0)
    rc3_src[...] = tile
    rc3 = [copy("rc3", d - 1, rc3_src, rc3_buf.at[d - 1], at_x(d)) for d in (1, 2, 3)]
    for one in rc3:
        one.start()
    for one in rc3:
        one.wait_recv()
    tile = rc3_src[...] + rc3_buf[0] + rc3_buf[1] + rc3_buf[2]
    for one in rs:
        one.wait_recv()
    value = hid[:ROWS, :]
    for d in range(3):
        value += rs_buf[d].astype(F32)
    for i in range(2):
        line = jnp.concatenate([tile[2 * j + i : 2 * j + i + 1, :] for j in range(4)], axis=1)
        here = iota((ROWS, D), 0) + x * ROWS == coarse_ref[0, i]
        value += jnp.where(here, line, 0.0)
    grad_ref[...] += dot_t(value.astype(BF16), weight(1))

    for one in c1 + list(w1.values()) + lat_copies + w2a + w2b + w3a + w3b:
        one.wait_send()
    for one in halo_copies + c3 + rc1 + hb + rs + rc3:
        one.wait_send()
    for d in order:
        c2(d).wait_send()
        rc2(d).wait_send()


def body(node, edge, weights, biases, gains, shifts, halo_send, halo_count, coarse, esend, erecv, cot):
    vmem = pl.BlockSpec(memory_space=pltpu.VMEM)
    smem = pl.BlockSpec(memory_space=pltpu.SMEM)
    return pl.pallas_call(
        kernel,
        name="layer",
        out_shape=(
            jax.ShapeDtypeStruct((ROWS, D), BF16),
            jax.ShapeDtypeStruct((ROWS, D), F32),
        ),
        in_specs=[smem, smem] + [vmem] * 10,
        out_specs=(vmem, vmem),
        scratch_shapes=[
            pltpu.VMEM((TABLE, D), BF16),
            pltpu.VMEM((TABLE, D), BF16),
            pltpu.VMEM((7, NX, 4, 2, 16, D), BF16),
            pltpu.VMEM((EDGES, TABLE), BF16),
            pltpu.VMEM((TABLE, EDGES), BF16),
            pltpu.VMEM((EDGES, BLOCK), BF16),
            pltpu.VMEM((2, BLOCK, SLOTS), BF16),
            pltpu.VMEM((EDGES, D), F32),
            pltpu.VMEM((EDGES, D), F32),
            pltpu.VMEM((EDGES, 1), F32),
            pltpu.VMEM((EDGES, D), BF16),
            pltpu.VMEM((EDGES, D), BF16),
            pltpu.VMEM((8, 128), F32),
            pltpu.VMEM((3, 8, 128), F32),
            pltpu.VMEM((8, 128), F32),
            pltpu.VMEM((NZ, 8, 128), F32),
            pltpu.VMEM((32, D), BF16),
            pltpu.VMEM((HALO, D), BF16),
            pltpu.VMEM((HALO, D), BF16),
            pltpu.VMEM((HALO, D), BF16),
            pltpu.VMEM((3, ROWS, D), BF16),
            pltpu.VMEM((3, ROWS, D), BF16),
            pltpu.VMEM((COARSE, D), BF16),
            pltpu.VMEM((7, 32, D), BF16),
            pltpu.VMEM((NZ, 8, 128), F32),
            pltpu.VMEM((NZ, 8, 128), F32),
            pltpu.VMEM((8, 128), F32),
            pltpu.VMEM((3, 8, 128), F32),
            pltpu.SemaphoreType.DMA((N_SEM,)),
            pltpu.SemaphoreType.DMA((N_SEM,)),
            pltpu.SemaphoreType.DMA((2,)),
        ],
        compiler_params=pltpu.CompilerParams(
            collective_id=0, has_side_effects=True, vmem_limit_bytes=50 * 2**20
        ),
    )(
        coarse, halo_count, node, edge, weights.reshape(7, 4, 2, 16, D), biases, gains, shifts,
        halo_send.reshape(1, HALO), esend.reshape(1, EDGES), erecv.reshape(1, EDGES), cot,
    )


def solution(mesh):
    rows = P(("dom", "feat"), None)
    flat = P(("dom", "feat"))
    return jax.shard_map(
        body,
        mesh=mesh,
        in_specs=(
            rows, rows, P(None, "feat", None), P(), P(), P(),
            P("dom", None, None), P("dom", None), P("dom", None), flat, flat, rows,
        ),
        out_specs=(rows, rows),
        check_vma=False,
    )
```

time: 642 us -> 81.5 us (0.13)
  waiting for transfers between devices: 412 us -> 0 us
  blocking collectives: 104 us -> 0 us
  Pallas kernels: 0 us -> 72.5 us
  other arithmetic: 33.8 us -> 0 us
  starting transfers between devices: 28.2 us -> 0 us
  matrix products: 22.4 us -> 0 us
  local copies, waits for them, and re-layouts: 24.1 us -> 7.92 us
  between operations: 15 us -> 0.68 us
    unnamed x5 -> x0, waiting for transfers between devices: 311 us -> none
    all_gather x1 -> x0, blocking collectives: 104 us -> none  [body(): coarse_table = lax.all_gather(coarse_mine, 'dom', axis=0, tiled=True)]
    all_gather x2 -> x0, waiting for transfers between devices: 73.4 us -> none  [the longest x1 51.4 us: body(): full_weights = lax.all_gather(weights, 'feat', axis=1, tiled=True)]
    pallas_call x0 -> x1, Pallas kernels: none -> 72.5 us  [body(): pl.pallas_call(kernel, name='layer', out_shape=(jax.ShapeDtypeStruct((ROW...]
    ppermute x8 -> x0, starting transfers between devices: 28.1 us -> none  [shifted(): return lax.ppermute(block, axis, route)]
    reduce_scatter x1 -> x0, waiting for transfers between devices: 24.4 us -> none  [body(): lax.psum_scatter(part_grad.astype(jnp.bfloat16), 'feat', scatter_dimensio...]
    dot_general x17 -> x0, matrix products: 22.4 us -> none  [the longest x13 17.5 us: product(): return jnp.dot(left, right, preferred_element_type=jnp.float32)]
    scatter-add x2 -> x0, other arithmetic: 12.2 us -> none  [the longest x1 8.8 us: body(): jax.ops.segment_sum(hidden_grad.astype(jnp.float32), edge_send, num_segme...]
  transfers between devices with their start and end apart: 12 -> 0, of which waited for: 5 -> 0; matrix products, arithmetic and copies ran while one was open for 6% -> 0% of each run, Pallas kernels for 0% -> 0%
where the time goes in v1:
time: 81.5 us; the launch traced here: 81.1 us
  Pallas kernels  72.5 us (89%)
  local copies, waits for them, and re-layouts  7.92 us (10%)
    pallas_call x1, Pallas kernels, body(): pl.pallas_call(kernel, name='layer', out_shape=(jax.ShapeDtypeStruct((ROW...  72.5 us
    unnamed x20, local copies, waits for them, and re-layouts  5.72 us

profile of v1, /device:TPU:1, one launch (start us, length us, event | category | flops | bytes accessed | tf_op | source)
XLA Modules:
  0.0 81.1 jit_solution(5020442561867475437)
XLA Ops:
  0.6 0.0 copy-start.4
  0.6 0.8 reshape.17.halo_ref
  1.4 0.0 copy-start.6
  1.4 0.7 reshape.18.esend_ref
  2.1 0.0 copy-start.5
  2.1 0.0 copy-start.7
  2.1 0.0 copy-start.8
  2.1 0.7 reshape.19.erecv_ref
  2.9 0.0 copy-done.4
  2.9 0.0 copy-done.6
  2.9 0.0 copy-done.5
  2.9 0.0 copy-done.7
  2.9 0.0 copy-done.8
  2.9 0.0 copy-start
  2.9 1.2 %copy-done = bf16[7,128,512]{2,1,0:T(8,128)(2,1)S(1)} copy-done((bf16[7,128,512]{2,1,0:T(8,128)(2,1)S(1)}, bf16[7,128,512]{2,1,0:T(8,128)(2,1)}, u32[]{:S(2)}) %copy-start) | copy-done | bytes 917528
  4.1 0.0 copy-start.1
  4.1 1.1 %copy-done.1 = bf16[768,512]{1,0:T(8,128)(2,1)S(1)} copy-done((bf16[768,512]{1,0:T(8,128)(2,1)S(1)}, bf16[768,512]{1,0:T(8,128)(2,1)}, u32[]{:S(2)}) %copy-start.1) | copy-done | bytes 786456
  5.2 0.0 copy-start.2
  5.2 0.9 %copy-done.2 = bf16[256,512]{1,0:T(8,128)(2,1)S(1)} copy-done((bf16[256,512]{1,0:T(8,128)(2,1)S(1)}, bf16[256,512]{1,0:T(8,128)(2,1)}, u32[]{:S(2)}) %copy-start.2) | copy-done | bytes 262168
  6.1 0.0 copy-start.3
  6.1 0.9 %copy-done.3 = bf16[256,512]{1,0:T(8,128)(2,1)S(1)} copy-done((bf16[256,512]{1,0:T(8,128)(2,1)S(1)}, bf16[256,512]{1,0:T(8,128)(2,1)}, u32[]{:S(2)}) %copy-start.3) | copy-done | bytes 262168
  7.1 72.5 %layer.1 = (bf16[256,512]{1,0:T(8,128)(2,1)S(1)}, f32[256,512]{1,0:T(8,128)S(1)}) custom-call(s32[1,2]{1,0:T(1,128)S(1)} %copy-done.7, s32[1,4]{1,0:T(1,128)S(1)} %copy-done.8, bf16[256,512]{1,0:T(8,128)(2,1)S(1)} %copy-done.2, bf16[768,512]{1,0:T(8,128)(2,1)S(1)} %copy-done.1, bf16[7,4,2,16,512]{4,3,2,1,0:T(8,128)(2,1)S(1)} %bitcast.1, ...), custom_call_target="tpu_custom_call" | custom-call | tf_op jit(solution)/shard_map/layer/pallas_call | solution.py:436
  79.7 0.7 copy.16
  80.4 0.8 copy.17
Async XLA Ops:
  0.6 2.2 %copy-start.4 = (f32[4,512]{1,0:T(4,128)S(1)}, f32[4,512]{1,0:T(4,128)}, u32[]{:S(2)}) copy-start(f32[4,512]{1,0:T(4,128)} %bias_ref.1) | copy-start | bytes 24580
  1.4 1.4 %copy-start.6 = (f32[2,512]{1,0:T(2,128)S(1)}, f32[2,512]{1,0:T(2,128)}, u32[]{:S(2)}) copy-start(f32[2,512]{1,0:T(2,128)} %shift_ref.1) | copy-start | bytes 12292
  2.1 0.7 copy-start.5
  2.1 0.7 copy-start.7
  2.1 0.8 copy-start.8
  2.9 1.2 %copy-start = (bf16[7,128,512]{2,1,0:T(8,128)(2,1)S(1)}, bf16[7,128,512]{2,1,0:T(8,128)(2,1)}, u32[]{:S(2)}) copy-start(bf16[7,128,512]{2,1,0:T(8,128)(2,1)} %param.14) | copy-start | bytes 2752516
  4.1 1.1 %copy-start.1 = (bf16[768,512]{1,0:T(8,128)(2,1)S(1)}, bf16[768,512]{1,0:T(8,128)(2,1)}, u32[]{:S(2)}) copy-start(bf16[768,512]{1,0:T(8,128)(2,1)} %edge_ref.1) | copy-start | bytes 2359300
  5.2 0.9 %copy-start.2 = (bf16[256,512]{1,0:T(8,128)(2,1)S(1)}, bf16[256,512]{1,0:T(8,128)(2,1)}, u32[]{:S(2)}) copy-start(bf16[256,512]{1,0:T(8,128)(2,1)} %node_ref.1) | copy-start | bytes 786436
  6.1 0.9 %copy-start.3 = (bf16[256,512]{1,0:T(8,128)(2,1)S(1)}, bf16[256,512]{1,0:T(8,128)(2,1)}, u32[]{:S(2)}) copy-start(bf16[256,512]{1,0:T(8,128)(2,1)} %cot_ref.1) | copy-start | bytes 786436

commit v2 on v1

--- a/solution.py
+++ b/solution.py
@@ -70,13 +70,14 @@
 
 
 def kernel(
-    coarse_ref, count_ref, node_ref, edge_ref, wsh_ref, bias_ref, gain_ref, shift_ref,
-    halo_ref, esend_ref, erecv_ref, cot_ref,
+    coarse_ref, count_ref, node_hbm, edge_hbm, wsh_ref, bias_hbm, gain_hbm, shift_hbm,
+    halo_hbm, esend_hbm, erecv_hbm, cot_hbm,
     out_ref, grad_ref,
-    lat, tab, w, sel, sel_t, rsel, rsel_t, hid, normed_e, inv_e, msg, hg,
+    node_ref, edge_ref, bias_ref, gain_ref, shift_ref, halo_ref, esend_ref, erecv_ref, cot_ref,
+    lat, tab, w, sel, sel_t, hsel, own_part, rsel, rsel_t, hid, normed_e, inv_e, msg, hg,
     c1_src, c1_buf, c2_src, c2_buf, c3_src, halo_src, hb_src, hb_buf, part_src, rs_buf,
     rc1_src, rc1_buf, rc2_src, rc2_buf, rc3_src, rc3_buf,
-    send_sem, recv_sem, local_sem,
+    send_sem, recv_sem, local_sem, met_sem,
 ):
     dom, x = lax.axis_index("dom"), lax.axis_index("feat")
     z, y, c = dom // 8, (dom // 2) % 4, dom % 2
@@ -115,11 +116,19 @@
     for o in OFFSETS:
         pl.semaphore_signal(barrier, inc=1, device_id=at_dom(o), device_id_type=MESH)
 
-    def greet(d, carry):
+    for d in (1, -1, 2, -2):
         pl.semaphore_signal(barrier, inc=1, device_id=at_z(d), device_id_type=MESH)
-        return carry
-
-    lax.fori_loop(1, NZ, greet, 0)
+
+    fetches = {}
+    pairs = dict(
+        node=(node_hbm, node_ref), halo=(halo_hbm, halo_ref), esend=(esend_hbm, esend_ref),
+        erecv=(erecv_hbm, erecv_ref), edge=(edge_hbm, edge_ref), cot=(cot_hbm, cot_ref),
+        bias=(bias_hbm, bias_ref), gain=(gain_hbm, gain_ref), shift=(shift_hbm, shift_ref),
+    )
+    for number, (name, (source, target)) in enumerate(pairs.items()):
+        fetches[name] = pltpu.make_async_copy(source, target, local_sem.at[2 + number])
+        fetches[name].start()
+    fetches["node"].wait()
 
     row8 = iota((8, ROWS), 0)
     wanted = jnp.where(row8 % 2 == 0, coarse_ref[0, 0], coarse_ref[0, 1]) - x * ROWS
@@ -132,7 +141,7 @@
 
     own_rows = pl.ds(pl.multiple_of(x * ROWS, ROWS), ROWS)
     lat[own_rows, :] = node_ref[...]
-    pl.semaphore_wait(barrier, 3 + 7 + 4 + 15)
+    pl.semaphore_wait(barrier, 3 + 7 + 4 + 4)
 
     c1 = [copy("c1", d - 1, c1_src, c1_buf.at[d - 1], at_x(d)) for d in (1, 2, 3)]
     for one in c1:
@@ -146,21 +155,19 @@
             for d in (2, 1, 3):
                 w1[g, t, d] = copy(
                     "w1", (g * 2 + t) * 3 + d - 1,
-                    wsh_ref.at[mats, j, c, :, cols], w.at[mats, x, j, c, :, cols], at_x(d),
+                    wsh_ref.at[mats, j, c, :, cols], w.at[mats, NX - d, j, c, :, cols], at_x(d),
                 )
                 w1[g, t, d].start()
-    lat_copies = [copy("lat", d - 1, node_ref, lat.at[own_rows, :], at_x(d)) for d in (2, 1, 3)]
+    lat_copies = [copy("lat", d - 1, node_hbm, lat.at[own_rows, :], at_x(d)) for d in (2, 1, 3)]
     for one in lat_copies:
         one.start()
-    for t, (j, _) in enumerate(pieces):
-        cols = pl.ds(256 * t, 256)
-        own = pltpu.make_async_copy(
-            wsh_ref.at[:, j, c, :, cols], w.at[:, x, j, c, :, cols], local_sem.at[t]
-        )
-        own.start()
-        own.wait()
-
-    halo_row = halo_ref[...]
+    for d in (2, -2):
+        pl.semaphore_signal(met_sem.at[0], inc=1, device_id=at_z(d), device_id_type=MESH)
+    own = pltpu.make_async_copy(wsh_ref, w.at[:, 0], local_sem.at[0])
+    own.start()
+
+    fetches["halo"].wait()
+    halo_row = jnp.concatenate([halo_ref[0, k : k + 1, :] for k in range(4)], axis=1)
     lane = iota((1, HALO), 1)
     live = count_ref[0, 0]
     for k in (1, 2, 3):
@@ -168,8 +175,13 @@
     halo_row = jnp.where(lane % 64 < live, halo_row, -1)
     halo_col = columns(halo_row)
 
+    pl.semaphore_wait(met_sem.at[0], 2)
+    for d in (4, -4):
+        pl.semaphore_signal(met_sem.at[1], inc=1, device_id=at_z(d), device_id_type=MESH)
+
     for one in c1:
         one.wait_recv()
+    pl.semaphore_wait(met_sem.at[1], 2)
     total = c1_src[...] + c1_buf[0] + c1_buf[1] + c1_buf[2]
     c2_src[...] = total
     c2_buf[z] = total
@@ -188,7 +200,8 @@
     for d in order:
         c2(d).start()
 
-    index = esend_ref[...]
+    fetches["esend"].wait()
+    index = esend_ref[...].reshape(1, EDGES)
     m = index - (PART + HALO)
     index = jnp.where(
         m >= 0, PART + HALO + ((m >> 1) & 7) * 32 + (m >> 4) * 2 + (m & 1), index
@@ -205,7 +218,7 @@
             for d in (2, 1, 3):
                 step = d if d < 3 else -1
                 target = at_y(d) if t == 0 else at_z(step)
-                part = w.at[mats, :, j, c, :, cols]
+                part = w.at[mats, pl.ds(1, 3), j, c, :, cols]
                 one = copy("w2", (g * 2 + t) * 3 + d - 1, part, part, target)
                 one.start()
                 started.append(one)
@@ -218,7 +231,7 @@
         for t in range(2):
             for one in arrived[3 * t : 3 * t + 3]:
                 one.wait_recv()
-            part = w.at[mats, :, :, c, :, pl.ds(256 * t, 256)]
+            part = w.at[mats, pl.ds(1, 3), :, c, :, pl.ds(256 * t, 256)]
             one = copy("w3", g * 2 + t, part, part, other_core)
             one.start()
             started.append(one)
@@ -229,7 +242,8 @@
     for j in range(TABLE // 128):
         sel[:, 128 * j : 128 * j + 128] = onehot(index_col == iota((EDGES, 128), 1) + 128 * j)
     w2b = w2_start(1)
-    recv_row = erecv_ref[...]
+    fetches["erecv"].wait()
+    recv_row = erecv_ref[...].reshape(1, EDGES)
     recv_col = columns(recv_row)
     rsel[...] = onehot(recv_col == iota((EDGES, 128), 1))
     for b in range(2):
@@ -237,24 +251,10 @@
             iota((BLOCK, SLOTS), 0) == recv_row[:, SLOTS * b : SLOTS * b + SLOTS]
         )
 
-    w3a = w3_start(0, w2a)
-    for one in lat_copies:
-        one.wait_recv()
-    chosen = jnp.zeros((HALO, D), F32)
-    for j in range(2):
-        pick = jnp.concatenate(
-            [onehot(halo_col == iota((HALO, 128), 1) + 128 * (4 * j + i)) for i in range(4)], axis=1
-        )
-        chosen += dot(pick, lat[512 * j : 512 * j + 512, :])
-    halo_src[...] = chosen.astype(BF16)
-    halo_copies = []
-    for k in range(4):
-        one = copy(
-            "halo", k, halo_src.at[pl.ds(64 * k, 64)], lat.at[pl.ds(PART + 64 * k, 64)], at_dom(OFFSETS[k])
-        )
-        one.start()
-        halo_copies.append(one)
-
+    for j in range(PART // 128):
+        hsel[:, 128 * j : 128 * j + 128] = onehot(halo_col == iota((HALO, 128), 1) + 128 * j)
+    for j in range(TABLE // 128):
+        sel_t[128 * j : 128 * j + 128, :] = onehot(iota((128, EDGES), 0) + 128 * j == index)
     for d in order:
         c2(d).wait_recv()
     flat = c2_buf[...].reshape(NZ * 8, 128).astype(BF16)
@@ -269,11 +269,29 @@
     c3 = [copy("c3", e - 1, c3_src, lat.at[coarse_rows, :], at_yc(e)) for e in range(1, 8)]
     for one in c3:
         one.start()
+    w3a = w3_start(0, w2a)
+    for one in lat_copies:
+        one.wait_recv()
+    halo_src[...] = dot(hsel[...], lat[:PART, :]).astype(BF16)
+    halo_copies = []
+    for k in range(4):
+        one = copy(
+            "halo", k, halo_src.at[pl.ds(64 * k, 64)], lat.at[pl.ds(PART + 64 * k, 64)], at_dom(OFFSETS[k])
+        )
+        one.start()
+        halo_copies.append(one)
+
     w3b = w3_start(1, w2b)
 
     def weight(i):
-        return w[i].reshape(D, D)
-
+        return jnp.concatenate(
+            [w[i, (k - x + NX) % NX].reshape(D // NX, D) for k in range(NX)], axis=0
+        )
+
+    own.wait()
+
+    for name in ("edge", "cot", "bias", "gain", "shift"):
+        fetches[name].wait()
     for one in w3a:
         one.wait_recv()
     w_e, w_s, w_r = weight(0), weight(1), weight(2)
@@ -289,15 +307,14 @@
             + dot(sel[rows, :PART], tab[:PART, :])
             + bias_ref[0:1, :]
         )
-    for j in range(TABLE // 128):
-        sel_t[128 * j : 128 * j + 128, :] = onehot(iota((128, EDGES), 0) + 128 * j == index)
+    for one in c3:
+        one.wait_recv()
+    rows = slice(PART + HALO, TABLE)
+    tab[rows, :] = dot(lat[rows, :], w_s).astype(BF16)
+    hid[...] += dot(sel[:, PART + HALO :], tab[rows, :])
     for one in halo_copies:
         one.wait_recv()
     rows = slice(PART, PART + HALO)
-    tab[rows, :] = dot(lat[rows, :], w_s).astype(BF16)
-    for one in c3:
-        one.wait_recv()
-    rows = slice(PART + HALO, TABLE)
     tab[rows, :] = dot(lat[rows, :], w_s).astype(BF16)
 
     for one in w3b:
@@ -305,7 +322,7 @@
     aggregate = []
     for b in range(2):
         rows = slice(SLOTS * b, SLOTS * b + SLOTS)
-        h = hid[rows, :] + dot(sel[rows, PART:], tab[PART:, :])
+        h = hid[rows, :] + dot(sel[rows, PART : PART + HALO], tab[PART : PART + HALO, :])
         hid[rows, :] = h
         act = (h * sigmoid(h)).astype(BF16)
         normed, inv = norm(dot(act, weight(3)) + bias_ref[1:2, :])
@@ -334,23 +351,26 @@
         s = sigmoid(h)
         hg[rows, :] = (dot_t(edge_back, weight(3)) * (s * (1.0 + h * (1.0 - s)))).astype(BF16)
 
-    rc1_src[...] = dot(sel_t[PART + HALO :, :], hg[...]).astype(BF16)
-    rc1 = [
-        copy(
-            "rc1", e - 1,
-            rc1_src.at[pl.ds(pl.multiple_of((yc + e) % 8 * 32, 32), 32)], rc1_buf.at[e - 1], at_yc(e),
-        )
-        for e in range(1, 8)
-    ]
-    for one in rc1:
-        one.start()
     hb_src[...] = dot(sel_t[PART : PART + HALO, :], hg[...]).astype(BF16)
     hb = []
     for k in range(4):
         part = pl.ds(64 * k, 64)
         hb.append(copy("hb", k, hb_src.at[part], hb_buf.at[part], at_dom(-OFFSETS[k])))
         hb[-1].start()
-
+    rc1_src[...] = dot(sel_t[PART + HALO :, :], hg[...]).astype(BF16)
+    rc1 = [
+        copy(
+            "rc1", e - 1,
+            rc1_src.at[pl.ds(pl.multiple_of((yc + e) % 8 * 32, 32), 32)], rc1_buf.at[e - 1], at_yc(e),
+        )
+        for e in range(1, 8)
+    ]
+    for one in rc1:
+        one.start()
+
+    starts = [pl.multiple_of(((x + d) % NX) * ROWS, ROWS) for d in range(NX)]
+    for d in (2, 1, 3, 0):
+        own_part[d] = dot(sel_t[pl.ds(starts[d], ROWS), :], hg[...])
     recv_grad = [
         dot(rsel_t[b], hg[SLOTS * b : SLOTS * b + SLOTS, :]).astype(BF16) for b in range(2)
     ]
@@ -359,6 +379,15 @@
         + dot_t(node_in_grad, weight(4))
         + dot_t(jnp.concatenate(recv_grad, axis=0), weight(2))
     )
+
+    for one in hb:
+        one.wait_recv()
+    rs = []
+    for d in (2, 1, 3):
+        place = onehot(iota((ROWS, HALO), 0) + starts[d] == halo_row)
+        part_src[d - 1] = (own_part[d] + dot(place, hb_buf[...])).astype(BF16)
+        rs.append(copy("rs", d - 1, part_src.at[d - 1], rs_buf.at[d - 1], at_x(d)))
+        rs[-1].start()
 
     for one in rc1:
         one.wait_recv()
@@ -385,20 +414,8 @@
     for d in order:
         rc2(d).start()
 
-    for one in hb:
-        one.wait_recv()
-    rs = []
-    for d in (2, 1, 3, 0):
-        start_row = pl.multiple_of(((x + d) % NX) * ROWS, ROWS)
-        chunk = pl.ds(start_row, ROWS)
-        place = onehot(iota((ROWS, HALO), 0) + start_row == halo_row)
-        value = dot(sel_t[chunk, :], hg[...]) + dot(place, hb_buf[...])
-        if d:
-            part_src[d - 1] = value.astype(BF16)
-            rs.append(copy("rs", d - 1, part_src.at[d - 1], rs_buf.at[d - 1], at_x(d)))
-            rs[-1].start()
-        else:
-            hid[:ROWS, :] = value
+    place = onehot(iota((ROWS, HALO), 0) + starts[0] == halo_row)
+    own_part[0] += dot(place, hb_buf[...])
 
     for d in order:
         rc2(d).wait_recv()
@@ -412,7 +429,7 @@
     tile = rc3_src[...] + rc3_buf[0] + rc3_buf[1] + rc3_buf[2]
     for one in rs:
         one.wait_recv()
-    value = hid[:ROWS, :]
+    value = own_part[0]
     for d in range(3):
         value += rs_buf[d].astype(F32)
     for i in range(2):
@@ -440,14 +457,25 @@
             jax.ShapeDtypeStruct((ROWS, D), BF16),
             jax.ShapeDtypeStruct((ROWS, D), F32),
         ),
-        in_specs=[smem, smem] + [vmem] * 10,
+        in_specs=[smem, smem] + [pl.BlockSpec(memory_space=pl.ANY)] * 10,
         out_specs=(vmem, vmem),
         scratch_shapes=[
+            pltpu.VMEM((ROWS, D), BF16),
+            pltpu.VMEM((EDGES, D), BF16),
+            pltpu.VMEM((4, D), F32),
+            pltpu.VMEM((2, D), F32),
+            pltpu.VMEM((2, D), F32),
+            pltpu.VMEM((1, 4, 64), jnp.int32),
+            pltpu.VMEM((EDGES,), jnp.int32),
+            pltpu.VMEM((EDGES,), jnp.int32),
+            pltpu.VMEM((ROWS, D), BF16),
             pltpu.VMEM((TABLE, D), BF16),
             pltpu.VMEM((TABLE, D), BF16),
             pltpu.VMEM((7, NX, 4, 2, 16, D), BF16),
             pltpu.VMEM((EDGES, TABLE), BF16),
             pltpu.VMEM((TABLE, EDGES), BF16),
+            pltpu.VMEM((HALO, PART), BF16),
+            pltpu.VMEM((NX, ROWS, D), F32),
             pltpu.VMEM((EDGES, BLOCK), BF16),
             pltpu.VMEM((2, BLOCK, SLOTS), BF16),
             pltpu.VMEM((EDGES, D), F32),
@@ -473,14 +501,15 @@
             pltpu.VMEM((3, 8, 128), F32),
             pltpu.SemaphoreType.DMA((N_SEM,)),
             pltpu.SemaphoreType.DMA((N_SEM,)),
-            pltpu.SemaphoreType.DMA((2,)),
+            pltpu.SemaphoreType.DMA((11,)),
+            pltpu.SemaphoreType.REGULAR((2,)),
         ],
         compiler_params=pltpu.CompilerParams(
-            collective_id=0, has_side_effects=True, vmem_limit_bytes=50 * 2**20
+            collective_id=0, has_side_effects=True, vmem_limit_bytes=60 * 2**20
         ),
     )(
         coarse, halo_count, node, edge, weights.reshape(7, 4, 2, 16, D), biases, gains, shifts,
-        halo_send.reshape(1, HALO), esend.reshape(1, EDGES), erecv.reshape(1, EDGES), cot,
+        halo_send, esend, erecv, cot,
     )
 
 

time: 81.5 us -> 68.6 us (0.84)
  Pallas kernels: 72.5 us -> 65.3 us
  local copies, waits for them, and re-layouts: 7.92 us -> 2.52 us
    pallas_call x1, Pallas kernels: 72.5 us -> 65.3 us  [body(): pl.pallas_call(kernel, name='layer', out_shape=(jax.ShapeDtypeStruct((ROW...]
    unnamed x20 -> x4, local copies, waits for them, and re-layouts: 5.72 us -> 2.52 us
    reshape x3 -> x0, local copies, waits for them, and re-layouts: 2.2 us -> none  [the longest x1 0.77 us: body(): halo_send.reshape(1, HALO)]
where the time goes in v2:
time: 68.6 us; the launch traced here: 68.4 us
  Pallas kernels  65.3 us (95%)
  local copies, waits for them, and re-layouts  2.52 us (4%)
    pallas_call x1, Pallas kernels, body(): pl.pallas_call(kernel, name='layer', out_shape=(jax.ShapeDtypeStruct((ROW...  65.3 us
    unnamed x4, local copies, waits for them, and re-layouts  2.52 us

profile of v2, /device:TPU:1, one launch (start us, length us, event | category | flops | bytes accessed | tf_op | source)
XLA Modules:
  0.0 68.4 jit_solution(9629946498043448437)
XLA Ops:
  0.6 65.3 %layer.1 = (bf16[256,512]{1,0:T(8,128)(2,1)}, f32[256,512]{1,0:T(8,128)}) custom-call(s32[1,2]{1,0:T(1,128)} %coarse_ref.1, s32[1,4]{1,0:T(1,128)} %count_ref.1, bf16[256,512]{1,0:T(8,128)(2,1)} %node_hbm.1, bf16[768,512]{1,0:T(8,128)(2,1)} %edge_hbm.1, bf16[7,4,2,16,512]{4,3,2,1,0:T(8,128)(2,1)} %bitcast.1, f32[4,512]{1,0:T(4,128)} %bias_hbm.1, ...), custom_call_target="tpu_custom_call" | custom-call | tf_op jit(solution)/shard_map/layer/pallas_call | solution.py:453
  65.9 0.0 copy-start
  65.9 1.7 %copy.16 = bf16[256,512]{1,0:T(8,128)(2,1)} copy(bf16[256,512]{1,0:T(8,128)(2,1)} %get-tuple-element.4) | data formatting | bytes 524288
  67.6 0.0 copy-done
  67.6 0.8 %copy.17 = f32[256,512]{1,0:T(8,128)} copy(f32[256,512]{1,0:T(8,128)S(1)} %copy-done) | data formatting | bytes 1048576
Async XLA Ops:
  65.9 1.7 %copy-start = (f32[256,512]{1,0:T(8,128)S(1)}, f32[256,512]{1,0:T(8,128)}, u32[]{:S(2)}) copy-start(f32[256,512]{1,0:T(8,128)} %get-tuple-element.5) | copy-start | bytes 1572868

commit v3 on v2

--- a/solution.py
+++ b/solution.py
@@ -21,7 +21,7 @@
 GROUPS = ((0, 3), (3, 4))
 EPS = 1e-05
 
-COUNTS = dict(c1=3, w1=12, lat=3, c2=15, w2=12, halo=4, w3=4, c3=7, hb=4, rs=3, rc1=7, rc2=15, rc3=3)
+COUNTS = dict(c1=3, w1=12, lat=3, c2=15, w2=12, halo=4, w3=4, c3=3, c3b=1, hb=4, rs=6, rca=1, rc1=3, rc2=15, rc3=3)
 BASE = {}
 _total = 0
 for _name, _n in COUNTS.items():
@@ -75,7 +75,7 @@
     out_ref, grad_ref,
     node_ref, edge_ref, bias_ref, gain_ref, shift_ref, halo_ref, esend_ref, erecv_ref, cot_ref,
     lat, tab, w, sel, sel_t, hsel, own_part, rsel, rsel_t, hid, normed_e, inv_e, msg, hg,
-    c1_src, c1_buf, c2_src, c2_buf, c3_src, halo_src, hb_src, hb_buf, part_src, rs_buf,
+    c1_src, c1_buf, c2_src, c2_buf, c3_src, halo_src, hb_src, hb_buf, part_src, rs_buf, far_buf, ctab, rca_buf, pair_sum, pair_src,
     rc1_src, rc1_buf, rc2_src, rc2_buf, rc3_src, rc3_buf,
     send_sem, recv_sem, local_sem, met_sem,
 ):
@@ -264,9 +264,8 @@
         parts.append(dot(onehot((row // 2) * 8 + 2 * j + row % 2 == iota((32, 128), 1)), flat))
     own_coarse = jnp.concatenate(parts, axis=1).astype(BF16)
     c3_src[...] = own_coarse
-    coarse_rows = pl.ds(pl.multiple_of(PART + HALO + yc * 32, 32), 32)
-    lat[coarse_rows, :] = own_coarse
-    c3 = [copy("c3", e - 1, c3_src, lat.at[coarse_rows, :], at_yc(e)) for e in range(1, 8)]
+    ctab[y, c] = own_coarse
+    c3 = [copy("c3", d - 1, c3_src, ctab.at[y, c], at_y(d)) for d in (2, 1, 3)]
     for one in c3:
         one.start()
     w3a = w3_start(0, w2a)
@@ -281,6 +280,10 @@
         one.start()
         halo_copies.append(one)
 
+    for one in c3:
+        one.wait_recv()
+    c3b = [copy("c3b", 0, ctab.at[:, c], ctab.at[:, c], other_core)]
+    c3b[0].start()
     w3b = w3_start(1, w2b)
 
     def weight(i):
@@ -307,10 +310,10 @@
             + dot(sel[rows, :PART], tab[:PART, :])
             + bias_ref[0:1, :]
         )
-    for one in c3:
+    for one in c3b:
         one.wait_recv()
     rows = slice(PART + HALO, TABLE)
-    tab[rows, :] = dot(lat[rows, :], w_s).astype(BF16)
+    tab[rows, :] = dot(ctab[...].reshape(COARSE, D), w_s).astype(BF16)
     hid[...] += dot(sel[:, PART + HALO :], tab[rows, :])
     for one in halo_copies:
         one.wait_recv()
@@ -357,20 +360,20 @@
         part = pl.ds(64 * k, 64)
         hb.append(copy("hb", k, hb_src.at[part], hb_buf.at[part], at_dom(-OFFSETS[k])))
         hb[-1].start()
-    rc1_src[...] = dot(sel_t[PART + HALO :, :], hg[...]).astype(BF16)
-    rc1 = [
-        copy(
-            "rc1", e - 1,
-            rc1_src.at[pl.ds(pl.multiple_of((yc + e) % 8 * 32, 32), 32)], rc1_buf.at[e - 1], at_yc(e),
-        )
-        for e in range(1, 8)
-    ]
-    for one in rc1:
-        one.start()
+    rc1_src[...] = dot(sel_t[PART + HALO :, :], hg[...]).astype(BF16).reshape(4, 2, 32, D)
+    rca = [copy("rca", 0, rc1_src.at[:, 1 - c], rca_buf, other_core)]
+    rca[0].start()
 
     starts = [pl.multiple_of(((x + d) % NX) * ROWS, ROWS) for d in range(NX)]
     for d in (2, 1, 3, 0):
         own_part[d] = dot(sel_t[pl.ds(starts[d], ROWS), :], hg[...])
+    for one in rca:
+        one.wait_recv()
+    pair_sum[...] = rc1_src[:, c].astype(F32) + rca_buf[...].astype(F32)
+    pair_src[...] = pair_sum[...].astype(BF16)
+    rc1 = [copy("rc1", d - 1, pair_src.at[(y + d) % NY], rc1_buf.at[d - 1], at_y(d)) for d in (2, 1, 3)]
+    for one in rc1:
+        one.start()
     recv_grad = [
         dot(rsel_t[b], hg[SLOTS * b : SLOTS * b + SLOTS, :]).astype(BF16) for b in range(2)
     ]
@@ -382,17 +385,37 @@
 
     for one in hb:
         one.wait_recv()
-    rs = []
-    for d in (2, 1, 3):
+    half = ROWS // 2
+
+    def with_halo(d):
         place = onehot(iota((ROWS, HALO), 0) + starts[d] == halo_row)
-        part_src[d - 1] = (own_part[d] + dot(place, hb_buf[...])).astype(BF16)
-        rs.append(copy("rs", d - 1, part_src.at[d - 1], rs_buf.at[d - 1], at_x(d)))
-        rs[-1].start()
+        return own_part[d] + dot(place, hb_buf[...])
+
+    low, high = pl.ds(0, half), pl.ds(half, half)
+
+    def rs_send(number, source, target, d):
+        one = copy("rs", number, source, target, at_x(d))
+        one.start()
+        return one
+
+    part_src[2] = with_halo(2).astype(BF16)
+    rs_far = [
+        rs_send(0, part_src.at[2, low], far_buf.at[0], 1),
+        rs_send(1, part_src.at[2, high], far_buf.at[1], 3),
+    ]
+    next_sum, last_sum = with_halo(1), with_halo(3)
+    own_part[1], own_part[3] = next_sum, last_sum
+    part_src[0, high] = next_sum[half:].astype(BF16)
+    part_src[1, low] = last_sum[:half].astype(BF16)
+    rs = [
+        rs_send(2, part_src.at[0, high], rs_buf.at[0, high], 1),
+        rs_send(3, part_src.at[1, low], rs_buf.at[1, low], 3),
+    ]
 
     for one in rc1:
         one.wait_recv()
-    gathered = rc1_src[pl.ds(pl.multiple_of(yc * 32, 32), 32), :].astype(F32)
-    for e in range(7):
+    gathered = pair_sum[y]
+    for e in range(3):
         gathered += rc1_buf[e].astype(F32)
     gathered = gathered.astype(BF16)
     spread = jnp.zeros((NZ * 8, 128), F32)
@@ -414,8 +437,13 @@
     for d in order:
         rc2(d).start()
 
-    place = onehot(iota((ROWS, HALO), 0) + starts[0] == halo_row)
-    own_part[0] += dot(place, hb_buf[...])
+    own_part[0] = with_halo(0)
+    for one in rs_far:
+        one.wait_recv()
+    part_src[0, low] = (own_part[1, low] + far_buf[0].astype(F32)).astype(BF16)
+    rs.append(rs_send(4, part_src.at[0, low], rs_buf.at[0, low], 1))
+    part_src[1, high] = (own_part[3, high] + far_buf[1].astype(F32)).astype(BF16)
+    rs.append(rs_send(5, part_src.at[1, high], rs_buf.at[1, high], 3))
 
     for d in order:
         rc2(d).wait_recv()
@@ -430,7 +458,7 @@
     for one in rs:
         one.wait_recv()
     value = own_part[0]
-    for d in range(3):
+    for d in range(2):
         value += rs_buf[d].astype(F32)
     for i in range(2):
         line = jnp.concatenate([tile[2 * j + i : 2 * j + i + 1, :] for j in range(4)], axis=1)
@@ -440,7 +468,7 @@
 
     for one in c1 + list(w1.values()) + lat_copies + w2a + w2b + w3a + w3b:
         one.wait_send()
-    for one in halo_copies + c3 + rc1 + hb + rs + rc3:
+    for one in halo_copies + c3 + c3b + rca + rc1 + hb + rs_far + rs + rc3:
         one.wait_send()
     for d in order:
         c2(d).wait_send()
@@ -492,9 +520,14 @@
             pltpu.VMEM((HALO, D), BF16),
             pltpu.VMEM((HALO, D), BF16),
             pltpu.VMEM((3, ROWS, D), BF16),
-            pltpu.VMEM((3, ROWS, D), BF16),
-            pltpu.VMEM((COARSE, D), BF16),
-            pltpu.VMEM((7, 32, D), BF16),
+            pltpu.VMEM((2, ROWS, D), BF16),
+            pltpu.VMEM((2, ROWS // 2, D), BF16),
+            pltpu.VMEM((4, 2, 32, D), BF16),
+            pltpu.VMEM((4, 32, D), BF16),
+            pltpu.VMEM((4, 32, D), F32),
+            pltpu.VMEM((4, 32, D), BF16),
+            pltpu.VMEM((4, 2, 32, D), BF16),
+            pltpu.VMEM((3, 32, D), BF16),
             pltpu.VMEM((NZ, 8, 128), F32),
             pltpu.VMEM((NZ, 8, 128), F32),
             pltpu.VMEM((8, 128), F32),

time: 68.6 us -> 66.6 us (0.971)
  Pallas kernels: 65.3 us -> 63.2 us
    pallas_call x1, Pallas kernels: 65.3 us -> 63.2 us  [body(): pl.pallas_call(kernel, name='layer', out_shape=(jax.ShapeDtypeStruct((ROW...]
where the time goes in v3:
time: 66.6 us; the launch traced here: 66.4 us
  Pallas kernels  63.2 us (95%)
  local copies, waits for them, and re-layouts  2.52 us (4%)
    pallas_call x1, Pallas kernels, body(): pl.pallas_call(kernel, name='layer', out_shape=(jax.ShapeDtypeStruct((ROW...  63.2 us
    unnamed x4, local copies, waits for them, and re-layouts  2.52 us

profile of v3, /device:TPU:1, one launch (start us, length us, event | category | flops | bytes accessed | tf_op | source)
XLA Modules:
  0.0 66.4 jit_solution(18288876955224475663)
XLA Ops:
  0.6 63.2 %layer.1 = (bf16[256,512]{1,0:T(8,128)(2,1)}, f32[256,512]{1,0:T(8,128)}) custom-call(s32[1,2]{1,0:T(1,128)} %coarse_ref.1, s32[1,4]{1,0:T(1,128)} %count_ref.1, bf16[256,512]{1,0:T(8,128)(2,1)} %node_hbm.1, bf16[768,512]{1,0:T(8,128)(2,1)} %edge_hbm.1, bf16[7,4,2,16,512]{4,3,2,1,0:T(8,128)(2,1)} %bitcast.1, f32[4,512]{1,0:T(4,128)} %bias_hbm.1, ...), custom_call_target="tpu_custom_call" | custom-call | tf_op jit(solution)/shard_map/layer/pallas_call | solution.py:481
  63.8 0.0 copy-start
  63.9 1.7 %copy.16 = bf16[256,512]{1,0:T(8,128)(2,1)} copy(bf16[256,512]{1,0:T(8,128)(2,1)} %get-tuple-element.4) | data formatting | bytes 524288
  65.6 0.0 copy-done
  65.6 0.8 %copy.17 = f32[256,512]{1,0:T(8,128)} copy(f32[256,512]{1,0:T(8,128)S(1)} %copy-done) | data formatting | bytes 1048576
Async XLA Ops:
  63.8 1.7 %copy-start = (f32[256,512]{1,0:T(8,128)S(1)}, f32[256,512]{1,0:T(8,128)}, u32[]{:S(2)}) copy-start(f32[256,512]{1,0:T(8,128)} %get-tuple-element.5) | copy-start | bytes 1572868

commit v4 on v3

--- a/solution.py
+++ b/solution.py
@@ -39,7 +39,7 @@
 
 
 def sigmoid(v):
-    return 1.0 / (1.0 + jnp.exp(-v))
+    return 0.5 + 0.5 * jnp.tanh(0.5 * v)
 
 
 def onehot(mask):
@@ -315,27 +315,29 @@
     rows = slice(PART + HALO, TABLE)
     tab[rows, :] = dot(ctab[...].reshape(COARSE, D), w_s).astype(BF16)
     hid[...] += dot(sel[:, PART + HALO :], tab[rows, :])
+    for one in w3b:
+        one.wait_recv()
+    node = node_ref[...]
+    own_part[0] = dot(node, weight(4)) + bias_ref[2:3, :]
     for one in halo_copies:
         one.wait_recv()
     rows = slice(PART, PART + HALO)
     tab[rows, :] = dot(lat[rows, :], w_s).astype(BF16)
 
-    for one in w3b:
-        one.wait_recv()
     aggregate = []
     for b in range(2):
         rows = slice(SLOTS * b, SLOTS * b + SLOTS)
         h = hid[rows, :] + dot(sel[rows, PART : PART + HALO], tab[PART : PART + HALO, :])
-        hid[rows, :] = h
-        act = (h * sigmoid(h)).astype(BF16)
+        s = sigmoid(h)
+        act = (h * s).astype(BF16)
+        hid[rows, :] = s * (1.0 + h * (1.0 - s))
         normed, inv = norm(dot(act, weight(3)) + bias_ref[1:2, :])
         normed_e[rows, :] = normed
         inv_e[rows, :] = inv
         msg[rows, :] = (normed * gain_ref[0:1, :] + shift_ref[0:1, :]).astype(BF16)
         aggregate.append(dot(rsel_t[b], msg[rows, :]).astype(BF16))
     aggregate = jnp.concatenate(aggregate, axis=0)
-    node = node_ref[...]
-    node_in = dot(node, weight(4)) + dot(aggregate, weight(5)) + bias_ref[2:3, :]
+    node_in = own_part[0] + dot(aggregate, weight(5))
     s = sigmoid(node_in)
     slope = s * (1.0 + node_in * (1.0 - s))
     normed, inv = norm(dot((node_in * s).astype(BF16), weight(6)) + bias_ref[3:4, :])
@@ -350,9 +352,7 @@
         rows = slice(SLOTS * b, SLOTS * b + SLOTS)
         back = dot(rsel[rows, :], agg_grad[BLOCK * b : BLOCK * b + BLOCK])
         edge_back = norm_back(back * gain_ref[0:1, :], normed_e[rows, :], inv_e[rows, :]).astype(BF16)
-        h = hid[rows, :]
-        s = sigmoid(h)
-        hg[rows, :] = (dot_t(edge_back, weight(3)) * (s * (1.0 + h * (1.0 - s)))).astype(BF16)
+        hg[rows, :] = (dot_t(edge_back, weight(3)) * hid[rows, :]).astype(BF16)
 
     hb_src[...] = dot(sel_t[PART : PART + HALO, :], hg[...]).astype(BF16)
     hb = []

time: 66.6 us -> 66.4 us (level)
  no operation moved by 1% of the time
where the time goes in v4:
time: 66.4 us; the launch traced here: 66.3 us
  Pallas kernels  63.1 us (95%)
  local copies, waits for them, and re-layouts  2.52 us (4%)
    pallas_call x1, Pallas kernels, body(): pl.pallas_call(kernel, name='layer', out_shape=(jax.ShapeDtypeStruct((ROW...  63.1 us
    unnamed x4, local copies, waits for them, and re-layouts  2.52 us

profile of v4, /device:TPU:1, one launch (start us, length us, event | category | flops | bytes accessed | tf_op | source)
XLA Modules:
  0.0 66.3 jit_solution(13909394103132142805)
XLA Ops:
  0.6 63.1 %layer.1 = (bf16[256,512]{1,0:T(8,128)(2,1)}, f32[256,512]{1,0:T(8,128)}) custom-call(s32[1,2]{1,0:T(1,128)} %coarse_ref.1, s32[1,4]{1,0:T(1,128)} %count_ref.1, bf16[256,512]{1,0:T(8,128)(2,1)} %node_hbm.1, bf16[768,512]{1,0:T(8,128)(2,1)} %edge_hbm.1, bf16[7,4,2,16,512]{4,3,2,1,0:T(8,128)(2,1)} %bitcast.1, f32[4,512]{1,0:T(4,128)} %bias_hbm.1, ...), custom_call_target="tpu_custom_call" | custom-call | tf_op jit(solution)/shard_map/layer/pallas_call | solution.py:481
  63.7 0.0 copy-start
  63.7 1.7 %copy.16 = bf16[256,512]{1,0:T(8,128)(2,1)} copy(bf16[256,512]{1,0:T(8,128)(2,1)} %get-tuple-element.4) | data formatting | bytes 524288
  65.5 0.0 copy-done
  65.5 0.8 %copy.17 = f32[256,512]{1,0:T(8,128)} copy(f32[256,512]{1,0:T(8,128)S(1)} %copy-done) | data formatting | bytes 1048576
Async XLA Ops:
  63.7 1.7 %copy-start = (f32[256,512]{1,0:T(8,128)S(1)}, f32[256,512]{1,0:T(8,128)}, u32[]{:S(2)}) copy-start(f32[256,512]{1,0:T(8,128)} %get-tuple-element.5) | copy-start | bytes 1572868

commit v5 on v4

--- a/solution.py
+++ b/solution.py
@@ -238,10 +238,10 @@
         return started
 
     w2a = w2_start(0)
+    w2b = w2_start(1)
     index_col = columns(index)
     for j in range(TABLE // 128):
         sel[:, 128 * j : 128 * j + 128] = onehot(index_col == iota((EDGES, 128), 1) + 128 * j)
-    w2b = w2_start(1)
     fetches["erecv"].wait()
     recv_row = erecv_ref[...].reshape(1, EDGES)
     recv_col = columns(recv_row)

time: 66.4 us -> 66.4 us (level)
  no operation moved by 1% of the time
where the time goes in v5:
time: 66.4 us; the launch traced here: 66.3 us
  Pallas kernels  63.1 us (95%)
  local copies, waits for them, and re-layouts  2.52 us (4%)
    pallas_call x1, Pallas kernels, body(): pl.pallas_call(kernel, name='layer', out_shape=(jax.ShapeDtypeStruct((ROW...  63.1 us
    unnamed x4, local copies, waits for them, and re-layouts  2.52 us

profile of v5, /device:TPU:1, one launch (start us, length us, event | category | flops | bytes accessed | tf_op | source)
XLA Modules:
  0.0 66.3 jit_solution(1603102982689895519)
XLA Ops:
  0.6 63.1 %layer.1 = (bf16[256,512]{1,0:T(8,128)(2,1)}, f32[256,512]{1,0:T(8,128)}) custom-call(s32[1,2]{1,0:T(1,128)} %coarse_ref.1, s32[1,4]{1,0:T(1,128)} %count_ref.1, bf16[256,512]{1,0:T(8,128)(2,1)} %node_hbm.1, bf16[768,512]{1,0:T(8,128)(2,1)} %edge_hbm.1, bf16[7,4,2,16,512]{4,3,2,1,0:T(8,128)(2,1)} %bitcast.1, f32[4,512]{1,0:T(4,128)} %bias_hbm.1, ...), custom_call_target="tpu_custom_call" | custom-call | tf_op jit(solution)/shard_map/layer/pallas_call | solution.py:481
  63.7 0.0 copy-start
  63.7 1.7 %copy.16 = bf16[256,512]{1,0:T(8,128)(2,1)} copy(bf16[256,512]{1,0:T(8,128)(2,1)} %get-tuple-element.4) | data formatting | bytes 524288
  65.5 0.0 copy-done
  65.5 0.8 %copy.17 = f32[256,512]{1,0:T(8,128)} copy(f32[256,512]{1,0:T(8,128)S(1)} %copy-done) | data formatting | bytes 1048576
Async XLA Ops:
  63.7 1.7 %copy-start = (f32[256,512]{1,0:T(8,128)S(1)}, f32[256,512]{1,0:T(8,128)}, u32[]{:S(2)}) copy-start(f32[256,512]{1,0:T(8,128)} %get-tuple-element.5) | copy-start | bytes 1572868
